TPU v7x, 256 devices: a whole 4x4x8 slice. The times are simulated.
256 devices in a mesh: user: 32 (over z, x), tp: 8 (over y, core).
Axes of the slice: x: 4, y: 4, z: 8, core: 2. Of those that a mesh axis runs over, the one named last changes fastest.
Arguments:
- cand_feats: bfloat16 [32768, 1024], P('user', 'tp'), may hold values from -6 to 6
- w_in: bfloat16 [1024, 2048], P(None, 'tp'), may hold values from -0.1875 to 0.1875
- w_out: bfloat16 [1024, 1024], P('tp'), may hold values from -0.1875 to 0.1875
- kv_cache: bfloat16 [2048, 128, 2048], P('user', None, 'tp'), may hold values from -6 to 6
- event_mask: int32 [2048, 128], P('user'), may hold values from 0 to 1, as said below
- block_counts: int32 [256], P('user'), may hold values from 1 to 8, as said below
- user_blocks: int32 [256, 8], P('user'), may hold values from 0 to 63, as said below
- send_slots: int32 [1024, 2], P('user'), may hold values from 0 to 63, as said below
- cand_user: int32 [32768], P('user'), may hold values from 0 to 7
Outputs:
- scored: bfloat16 [32768, 1024], P('user', 'tp')
Inputs may be any that keep to these rules, and one draw needn't show every extreme that they name: `block_counts`: on every index of the user axis some user has 8 blocks, and on one index every user has. For user u of the index r of the user axis and j < block_counts[r * 8 + u], user_blocks[r * 8 + u, j] = o * 2 + c says that block j of u's history is cached on index o, in its local row send_slots[o * 32 + r, c] of kv_cache and event_mask. These valid entries of one index's users are all different, and on one index they take all 64 values. Entries with j >= block_counts[u] are arbitrary. `send_slots`: the 32 rows of one holder o (rows o * 32 to o * 32 + 31) name each of its local rows 0 to 63 exactly once. `event_mask`: in every block of a user's history the first event is real.
All inputs are finite; a program needn't handle non-finite values.
Results may differ from a plain program's by a relative error of at most 0.013.
Values may be sent and summed in bfloat16 or wider, within the bound.
A program may use at most 128 MiB of HBM per device.

v0:
```python
import jax
import jax.numpy as jnp
from jax import lax
from jax.sharding import PartitionSpec as P

DH = 128
EVENTS = 128
norm_eps = 1e-06


def owner_users(block_count, block_table, slot_count):
    user_count, most_blocks = block_table.shape
    live_mask = jnp.arange(most_blocks, dtype=jnp.int32)[None, :] < block_count[:, None]
    slot_hit = (
        block_table[:, :, None] == jnp.arange(slot_count, dtype=jnp.int32)[None, None, :]
    ) & live_mask[:, :, None]
    user_label = jnp.arange(user_count, dtype=jnp.int32)[:, None, None] + 1
    return jnp.sum(jnp.where(slot_hit, user_label, 0), axis=(0, 1)) - 1


def attend(queries, users, key_pairs, marks, owners):
    row_count, heads_here = (queries.shape[0], queries.shape[1])
    block_rows = min(512, row_count)
    pair_rows = key_pairs.reshape(-1, heads_here, 2, DH)
    key_rows = pair_rows[:, :, 0, :]
    value_rows = pair_rows[:, :, 1, :]
    live_mask = marks.reshape(-1, EVENTS).astype(jnp.float32)
    owner_label = owners.astype(jnp.float32)

    def one_block(packed):
        query_block, user_block = packed
        same_user = (user_block.astype(jnp.float32)[:, None] == owner_label[None, :]).astype(
            jnp.float32
        )
        weights = (same_user[:, :, None] * live_mask[None]).reshape(query_block.shape[0], -1)
        scores = jnp.einsum(
            "rhd,ehd->hre", query_block, key_rows, preferred_element_type=jnp.float32
        ) * DH ** (-0.5)
        attn_weights = (jax.nn.silu(scores) * weights[None]).astype(jnp.bfloat16)
        return jnp.einsum(
            "hre,ehd->rhd", attn_weights, value_rows, preferred_element_type=jnp.float32
        )

    result = lax.map(
        one_block, (queries.reshape(-1, block_rows, heads_here, DH), users.reshape(-1, block_rows))
    )
    return result.reshape(row_count, heads_here, DH)


def per_device(
    cand_feats, w_in, w_out, kv_cache, event_mask, block_counts, user_blocks, send_slots, cand_user
):
    row_count = cand_feats.shape[0]
    heads_here = w_out.shape[0] // DH
    projected = jnp.dot(
        lax.all_gather(cand_feats, "tp", axis=1, tiled=True),
        w_in,
        preferred_element_type=jnp.float32,
    )
    activated = jax.nn.silu(projected).reshape(row_count, heads_here, 2, DH)
    queries = activated[:, :, 0, :].astype(jnp.bfloat16)
    gates = activated[:, :, 1, :].astype(jnp.bfloat16)
    peer_count = lax.axis_size("user")
    capacity = send_slots.shape[1]
    slot_users = owner_users(block_counts, user_blocks, peer_count * capacity)
    picked = send_slots.reshape(-1)
    outgoing = kv_cache[picked].reshape(peer_count, capacity, EVENTS, kv_cache.shape[2])
    out_marks = event_mask[picked].reshape(peer_count, capacity, EVENTS).astype(jnp.bfloat16)
    arrived, arrived_marks = (
        lax.all_to_all(outgoing, "user", split_axis=0, concat_axis=0, tiled=True),
        lax.all_to_all(out_marks, "user", split_axis=0, concat_axis=0, tiled=True),
    )
    attended = attend(queries, cand_user, arrived, arrived_marks, slot_users)
    normed = (
        attended
        * lax.rsqrt(jnp.mean(attended * attended, axis=-1, keepdims=True) + norm_eps)
        * gates.astype(jnp.float32)
    )
    hidden = normed.astype(jnp.bfloat16).reshape(row_count, heads_here * DH)
    head_terms = jnp.dot(hidden, w_out, preferred_element_type=jnp.float32)
    summed = lax.psum_scatter(
        head_terms.astype(jnp.bfloat16), "tp", scatter_dimension=1, tiled=True
    ).astype(jnp.float32)
    return (cand_feats.astype(jnp.float32) + summed).astype(jnp.bfloat16)


def solution(mesh):
    in_specs = (
        P("user", "tp"),
        P(None, "tp"),
        P("tp", None),
        P("user", None, "tp"),
        P("user", None),
        P("user"),
        P("user", None),
        P("user", None),
        P("user"),
    )
    out_specs = P("user", "tp")
    return jax.shard_map(
        per_device, mesh=mesh, in_specs=in_specs, out_specs=out_specs, check_vma=False
    )
```

profile of v0, /device:TPU:2, one launch (start us, length us, event | category | flops | bytes accessed | tf_op | source)
XLA Modules:
  0.0 248.5 jit_solution(2677720347667687180)
XLA Ops:
  6.5 0.0 copy-start
  6.5 0.8 copy.22
  7.4 0.1 reshape.201
  7.5 1.4 gather_fusion.1
  8.8 0.6 convert_element_type.84
  9.5 11.6 %all-to-all-start.1 = ((bf16[32,2,128]{2,1,0:T(2,128)(2,1)}), bf16[32,2,128]{2,1,0:T(2,128)(2,1)S(1)}, u32[]{:S(2)}, u32[]{:S(2)}) async-start(bf16[32,2,128]{2,1,0:T(2,128)(2,1)} %bitcast.14), calls=%async_computation.1 | async-start | bytes 32768 | tf_op jit(solution)/shard_map/all_to_all | solution.py:71
  21.1 5.0 %gather_fusion = bf16[64,128,256]{2,1,0:T(8,128)(2,1)} fusion(bf16[64,128,256]{2,1,0:T(8,128)(2,1)} %param.14, s32[1024]{0:T(1024)S(1)} %pad_clamp_fusion), kind=kCustom, calls=%fused_computation | custom fusion | bytes 8388864 | tf_op jit(solution)/shard_map/gather | solution.py:67
  26.0 3.5 %all-to-all-done.1 = bf16[32,2,128]{2,1,0:T(2,128)(2,1)S(1)} async-done(((bf16[32,2,128]{2,1,0:T(2,128)(2,1)}), bf16[32,2,128]{2,1,0:T(2,128)(2,1)S(1)}, u32[]{:S(2)}, u32[]{:S(2)}) %all-to-all-start.1) | async-done | bytes 16416 | tf_op jit(solution)/shard_map/all_to_all | solution.py:71
  29.5 0.0 copy-start.5
  29.5 0.0 copy-start.6
  29.5 0.0 copy-start.4
  29.5 6.5 %all-to-all-start = ((bf16[32,2,128,256]{3,2,1,0:T(8,128)(2,1)}), bf16[32,2,128,256]{3,2,1,0:T(8,128)(2,1)}, u32[]{:S(2)}, u32[]{:S(2)}) async-start(bf16[32,2,128,256]{3,2,1,0:T(8,128)(2,1)} %bitcast.92), calls=%async_computation | async-start | bytes 8388608 | tf_op jit(solution)/shard_map/all_to_all | solution.py:70
  36.0 0.0 all-gather.2.cloned.1.call-start
  36.1 0.7 all-gather.2.cloned.1.call-update
  36.8 0.0 reduce-scatter.4.cloned.1.call-start
  36.8 0.0 copy-done.5
  36.9 0.0 copy-done.6
  36.9 0.1 iota_compare_fusion.1
  37.0 0.0 copy-done.4
  37.0 0.1 select_reduce_fusion
  37.1 32.6 %all-gather.2.cloned.1.call-done = bf16[1024,1024]{1,0:T(8,128)(2,1)} async-done(((bf16[1024,128]{1,0:T(8,128)(2,1)}), bf16[1024,1024]{1,0:T(8,128)(2,1)}) %all-gather.2.cloned.1.call-update) | async-done | bytes 2097168 | tf_op jit(solution)/shard_map/all_gather | solution.py:56
  69.7 0.0 copy-done
  69.7 2.5 %multiply_convert_fusion = bf16[1024,256]{0,1:T(8,128)(2,1)S(1)} fusion(bf16[1024,1024]{1,0:T(8,128)(2,1)} %all-gather.2.cloned.1.call-done, bf16[1024,256]{1,0:T(8,128)(2,1)S(1)} %copy-done), kind=kOutput, calls=%fused_computation.20 | convolution fusion | flops 538181632 | bytes 3145728 | tf_op jit(solution)/shard_map/dot_general | solution.py:55
  72.2 0.0 copy-start.2
  72.2 0.8 copy-done.2
  73.0 0.8 copy.29
  73.8 55.0 %all-to-all-done = bf16[32,2,128,256]{3,2,1,0:T(8,128)(2,1)} async-done(((bf16[32,2,128,256]{3,2,1,0:T(8,128)(2,1)}), bf16[32,2,128,256]{3,2,1,0:T(8,128)(2,1)}, u32[]{:S(2)}, u32[]{:S(2)}) %all-to-all-start) | async-done | bytes 4194336 | tf_op jit(solution)/shard_map/all_to_all | solution.py:70
  128.9 7.0 %reshape.203 = bf16[8192,1,2,128]{3,2,0,1:T(2,128)(2,1)} reshape(bf16[32,2,128,256]{3,2,1,0:T(8,128)(2,1)} %all-to-all-done) | data formatting | bytes 8388608 | tf_op jit(solution)/shard_map/reshape | solution.py:24
  135.8 8.9 %fusion.29 = (bf16[8192,1,1,128]{3,2,0,1:T(2,128)(2,1)S(1)}, bf16[8192,1,1,128]{3,2,0,1:T(2,128)(2,1)S(1)}) fusion(bf16[8192,1,2,128]{3,2,0,1:T(2,128)(2,1)} %reshape.203), kind=kLoop, calls=%fused_computation.37 | loop fusion | bytes 8388608 | tf_op jit(solution)/shard_map/slice | solution.py:26
  144.7 1.9 copy_bitcast_fusion
  146.6 0.0 copy-start.3
  146.6 53.2 %while.10 = (s32[]{:T(128)}, f32[2,512,1,128]{3,1,2,0:T(8,128)S(1)}, bf16[2,512,1,128]{3,1,2,0:T(8,128)(2,1)}, bf16[8192,1,128]{2,0,1:T(8,128)(2,1)}, s32[2,512]...) while((s32[]{:T(128)}, ...), condition=%wide.region_2.3_spmd, body=%wide.region_1.2_spmd.sunk | while | flops 2181104128 | bytes 38444384 | solution.py:44
  146.6 0.1 compare_convert_fusion.2
  146.8 7.0 %mul.127 = f32[512,64,128]{2,1,0:T(8,128)} broadcast(f32[512,64]{1,0:T(8,128)S(1)} %compare_convert_fusion.2), dimensions={0,1} | broadcast | bytes 16908288 | tf_op jit(solution)/shard_map/while/body/eval_jaxpr/mul | solution.py:35
  153.8 19.4 %fusion.40 = f32[2,512,1,128]{3,1,2,0:T(8,128)S(1)} fusion(f32[2,512,1,128]{3,1,2,0:T(8,128)S(1)} %get-tuple-element.151, s32[]{:T(128)} %get-tuple-element.150, bf16[8192,1,128]{2,0,1:T(8,128)(2,1)S(1)} %get-tuple-element.166, f32[64,8,64,128]{3,2,1,0:T(8,128)} %bitcast.91, f32[8192]{0:T(1024)S(1)} %bitcast.101, ...), kind=kOutput, calls=%fused_computation.9.clone.1 | convolution fusion | flops 2181038080 | bytes 21398528 | tf_op jit(solution)/shard_map/while/body/eval_jaxpr/hre,ehd->rhd/dot_general | solution.py:40
  173.2 0.1 compare_convert_fusion.2
  173.4 7.0 %mul.127 = f32[512,64,128]{2,1,0:T(8,128)} broadcast(f32[512,64]{1,0:T(8,128)S(1)} %compare_convert_fusion.2), dimensions={0,1} | broadcast | bytes 16908288 | tf_op jit(solution)/shard_map/while/body/eval_jaxpr/mul | solution.py:35
  180.4 19.4 %fusion.40 = f32[2,512,1,128]{3,1,2,0:T(8,128)S(1)} fusion(f32[2,512,1,128]{3,1,2,0:T(8,128)S(1)} %get-tuple-element.151, s32[]{:T(128)} %get-tuple-element.150, bf16[8192,1,128]{2,0,1:T(8,128)(2,1)S(1)} %get-tuple-element.166, f32[64,8,64,128]{3,2,1,0:T(8,128)} %bitcast.91, f32[8192]{0:T(1024)S(1)} %bitcast.101, ...), kind=kOutput, calls=%fused_computation.9.clone.1 | convolution fusion | flops 2181038080 | bytes 21398528 | tf_op jit(solution)/shard_map/while/body/eval_jaxpr/hre,ehd->rhd/dot_general | solution.py:40
  199.8 0.2 multiply_reduce_fusion
  200.1 0.2 copy.24
  200.3 0.0 copy-done.3
  200.3 1.7 convolution_convert_fusion
  202.0 0.0 copy-start.1
  202.0 2.6 %copy.25 = bf16[1024,1024]{0,1:T(8,128)(2,1)} copy(bf16[1024,1024]{1,0:T(8,128)(2,1)S(1)} %convolution_convert_fusion) | data formatting | bytes 4194304
  204.6 0.0 reduce-scatter.4.cloned.1.call-update
  204.6 35.1 %reduce-scatter.4.cloned.1.call-done = bf16[128,1024]{1,0:T(8,128)(2,1)} async-done(((bf16[1024,1024]{1,0:T(8,128)(2,1)}), bf16[128,1024]{1,0:T(8,128)(2,1)}) %reduce-scatter.4.cloned.1.call-update) | async-done | bytes 262160
  239.8 1.1 copy.26
  240.9 0.0 copy-done.1
  240.9 0.8 add_convert_fusion
  (12 shorter events, 0.1 us)
Async XLA Ops:
  6.5 63.1 %copy-start = (bf16[1024,256]{1,0:T(8,128)(2,1)S(1)}, bf16[1024,256]{1,0:T(8,128)(2,1)}, u32[]{:S(2)}) copy-start(bf16[1024,256]{1,0:T(8,128)(2,1)} %param.12) | copy-start | bytes 1572868
  9.5 20.1 %all-to-all-start.1 = ((bf16[32,2,128]{2,1,0:T(2,128)(2,1)}), bf16[32,2,128]{2,1,0:T(2,128)(2,1)S(1)}, u32[]{:S(2)}, u32[]{:S(2)}) async-start(bf16[32,2,128]{2,1,0:T(2,128)(2,1)} %bitcast.14), calls=%async_computation.1 | async-start | bytes 32768 | tf_op jit(solution)/shard_map/all_to_all | solution.py:71
  29.5 7.3 %copy-start.5 = (s32[1024]{0:T(1024)S(1)}, s32[1024]{0:T(1024)}, u32[]{:S(2)}) copy-start(s32[1024]{0:T(1024)} %param.19) | copy-start | bytes 12292
  29.5 7.3 %copy-start.6 = (s32[8]{0:T(128)S(1)}, s32[8]{0:T(128)}, u32[]{:S(2)}) copy-start(s32[8]{0:T(128)} %param.16) | copy-start | bytes 100
  29.5 7.4 %copy-start.4 = (s32[8,8]{1,0:T(8,128)S(1)}, s32[8,8]{1,0:T(8,128)}, u32[]{:S(2)}) copy-start(s32[8,8]{1,0:T(8,128)} %param.17) | copy-start | bytes 772
  29.5 99.3 %all-to-all-start = ((bf16[32,2,128,256]{3,2,1,0:T(8,128)(2,1)}), bf16[32,2,128,256]{3,2,1,0:T(8,128)(2,1)}, u32[]{:S(2)}, u32[]{:S(2)}) async-start(bf16[32,2,128,256]{3,2,1,0:T(8,128)(2,1)} %bitcast.92), calls=%async_computation | async-start | bytes 8388608 | tf_op jit(solution)/shard_map/all_to_all | solution.py:70
  36.0 33.6 %all-gather.2.cloned.1.call-start = ((), (), s32[]{:S(2)}) async-start(), calls=%async_computation.3 | async-start | bytes 2359296 | tf_op jit(solution)/shard_map/all_gather | solution.py:56
  36.8 203.0 %reduce-scatter.4.cloned.1.call-start = ((), (), s32[]{:S(2)}) async-start(), calls=%async_computation.4 | async-start | bytes 2359296
  72.2 0.8 copy-start.2
  146.6 53.7 %copy-start.3 = (bf16[128,1024]{1,0:T(8,128)(2,1)S(1)}, bf16[128,1024]{1,0:T(8,128)(2,1)}, u32[]{:S(2)}) copy-start(bf16[128,1024]{1,0:T(8,128)(2,1)} %param.13) | copy-start | bytes 786436
  202.0 38.9 %copy-start.1 = (bf16[1024,128]{1,0:T(8,128)(2,1)S(1)}, bf16[1024,128]{1,0:T(8,128)(2,1)}, u32[]{:S(2)}) copy-start(bf16[1024,128]{1,0:T(8,128)(2,1)} %param.11) | copy-start | bytes 786436
Sparse Core Ops, SparseCore 0:
  38.7 30.9 all-gather.1
  204.7 34.9 reduce-scatter.3
where the time goes:
time: 249 us
  waiting for transfers between devices  127 us (51%)
  local copies, waits for them, and re-layouts  44.6 us (18%)
  matrix products  43 us (17%)
  starting transfers between devices  18.2 us (7%)
  between operations  13.6 us (5%)
    all_to_all x1, waiting for transfers between devices, per_device(): lax.all_to_all(outgoing, 'user', split_axis=0, concat_axis=0, tiled=True)  55 us
    dot_general x2, matrix products, one_block(): jnp.einsum('hre,ehd->rhd', attn_weights, value_rows, preferred_element_ty...  38.9 us
    unnamed x3, waiting for transfers between devices  35.8 us
    all_gather x1, waiting for transfers between devices, per_device(): lax.all_gather(cand_feats, 'tp', axis=1, tiled=True)  32.6 us
    mul x2, local copies, waits for them, and re-layouts, one_block(): same_user[:, :, None] * live_mask[None]  14 us
    all_to_all x1, starting transfers between devices, per_device(): lax.all_to_all(out_marks, 'user', split_axis=0, concat_axis=0, tiled=True)  11.6 us
    slice x1, local copies, waits for them, and re-layouts, attend(): value_rows = pair_rows[:, :, 1, :]  8.89 us
    unnamed x20, local copies, waits for them, and re-layouts  8.03 us
  transfers between devices with their start and end apart: 4, of which 4 were waited for; matrix products, arithmetic and copies ran while one was open for 3% of the time, Pallas kernels for 0%

commit v1 on v0

--- a/solution.py
+++ b/solution.py
@@ -53,7 +53,9 @@
     row_count = cand_feats.shape[0]
     heads_here = w_out.shape[0] // DH
     projected = jnp.dot(
-        lax.all_gather(cand_feats, "tp", axis=1, tiled=True),
+        jnp.concatenate(
+            lax.all_to_all(jnp.stack([cand_feats] * lax.axis_size("tp")), "tp", 0, 0), axis=1
+        ),
         w_in,
         preferred_element_type=jnp.float32,
     )

time: 249 us -> 282 us (1.13)
  waiting for transfers between devices: 127 us -> 154 us
  starting transfers between devices: 18.2 us -> 22.1 us
  local copies, waits for them, and re-layouts: 44.6 us -> 48 us
    all_to_all x1, waiting for transfers between devices: 55 us -> 93.9 us  [per_device(): lax.all_to_all(outgoing, 'user', split_axis=0, concat_axis=0, tiled=True)]
    all_gather x1 -> x0, waiting for transfers between devices: 32.6 us -> none  [per_device(): lax.all_gather(cand_feats, 'tp', axis=1, tiled=True)]
    all_to_all x0 -> x1, waiting for transfers between devices: none -> 22.2 us  [per_device(): lax.all_to_all(jnp.stack([cand_feats] * lax.axis_size('tp')), 'tp', 0, 0)]
    unnamed x3 -> x2, waiting for transfers between devices: 35.8 us -> 30.2 us
    all_to_all x0 -> x1, starting transfers between devices: none -> 4.47 us  [per_device(): lax.all_to_all(jnp.stack([cand_feats] * lax.axis_size('tp')), 'tp', 0, 0)]
    all_to_all x1, waiting for transfers between devices: 3.48 us -> 7.35 us  [per_device(): lax.all_to_all(out_marks, 'user', split_axis=0, concat_axis=0, tiled=True)]
    unnamed x20 -> x21, local copies, waits for them, and re-layouts: 8.03 us -> 9.12 us
where the time goes in v1:
time: 282 us; the launch traced here: 281 us
  waiting for transfers between devices  154 us (55%)
  local copies, waits for them, and re-layouts  48 us (17%)
  matrix products  41.6 us (15%)
  starting transfers between devices  22.1 us (8%)
  between operations  13.6 us (5%)
    all_to_all x1, waiting for transfers between devices, per_device(): lax.all_to_all(outgoing, 'user', split_axis=0, concat_axis=0, tiled=True)  93.9 us
    dot_general x2, matrix products, one_block(): jnp.einsum('hre,ehd->rhd', attn_weights, value_rows, preferred_element_ty...  38.9 us
    unnamed x2, waiting for transfers between devices  30.2 us
    all_to_all x1, waiting for transfers between devices, per_device(): lax.all_to_all(jnp.stack([cand_feats] * lax.axis_size('tp')), 'tp', 0, 0)  22.2 us
    mul x2, local copies, waits for them, and re-layouts, one_block(): same_user[:, :, None] * live_mask[None]  14.1 us
    all_to_all x1, starting transfers between devices, per_device(): lax.all_to_all(out_marks, 'user', split_axis=0, concat_axis=0, tiled=True)  11.6 us
    unnamed x21, local copies, waits for them, and re-layouts  9.12 us
    slice x1, local copies, waits for them, and re-layouts, attend(): value_rows = pair_rows[:, :, 1, :]  8.82 us
  transfers between devices with their start and end apart: 4, of which 4 were waited for; matrix products, arithmetic and copies ran while one was open for 3% of the time, Pallas kernels for 0%

profile of v1, /device:TPU:2, one launch (start us, length us, event | category | flops | bytes accessed | tf_op | source)
XLA Modules:
  0.0 281.2 jit_solution(5782591521710516762)
XLA Ops:
  6.5 0.0 copy-start
  6.5 0.8 copy.25
  7.4 0.1 reshape.211
  7.5 1.4 gather_fusion.1
  8.8 0.6 convert_element_type.84
  9.5 11.6 %all-to-all-start.2 = ((bf16[32,2,128]{2,1,0:T(2,128)(2,1)}), bf16[32,2,128]{2,1,0:T(2,128)(2,1)S(1)}, u32[]{:S(2)}, u32[]{:S(2)}) async-start(bf16[32,2,128]{2,1,0:T(2,128)(2,1)} %bitcast.16), calls=%async_computation.2 | async-start | bytes 32768 | tf_op jit(solution)/shard_map/all_to_all | solution.py:73
  21.1 1.1 copy.23
  22.2 7.4 %all-to-all-done.2 = bf16[32,2,128]{2,1,0:T(2,128)(2,1)S(1)} async-done(((bf16[32,2,128]{2,1,0:T(2,128)(2,1)}), bf16[32,2,128]{2,1,0:T(2,128)(2,1)S(1)}, u32[]{:S(2)}, u32[]{:S(2)}) %all-to-all-start.2) | async-done | bytes 16416 | tf_op jit(solution)/shard_map/all_to_all | solution.py:73
  29.5 1.6 stack.2
  31.1 4.5 %all-to-all-start = ((bf16[8,1024,128]{1,2,0:T(8,128)(2,1)}), bf16[8,1024,128]{1,2,0:T(8,128)(2,1)S(1)}, u32[]{:S(2)}, u32[]{:S(2)}) async-start(bf16[8,1024,128]{1,2,0:T(8,128)(2,1)} %stack.2), calls=%async_computation | async-start | bytes 4194304 | tf_op jit(solution)/shard_map/all_to_all | solution.py:57
  35.6 5.0 %gather_fusion = bf16[64,128,256]{2,1,0:T(8,128)(2,1)} fusion(bf16[64,128,256]{2,1,0:T(8,128)(2,1)} %param.14, s32[1024]{0:T(1024)S(1)} %pad_clamp_fusion), kind=kCustom, calls=%fused_computation | custom fusion | bytes 8388864 | tf_op jit(solution)/shard_map/gather | solution.py:69
  40.6 22.2 %all-to-all-done = bf16[8,1024,128]{1,2,0:T(8,128)(2,1)S(1)} async-done(((bf16[8,1024,128]{1,2,0:T(8,128)(2,1)}), bf16[8,1024,128]{1,2,0:T(8,128)(2,1)S(1)}, u32[]{:S(2)}, u32[]{:S(2)}) %all-to-all-start) | async-done | bytes 2097184 | tf_op jit(solution)/shard_map/all_to_all | solution.py:57
  62.8 0.0 copy-start.5
  62.8 0.0 copy-start.6
  62.8 0.0 copy-start.4
  62.8 6.0 %all-to-all-start.1 = ((bf16[32,2,128,256]{3,2,1,0:T(8,128)(2,1)}), bf16[32,2,128,256]{3,2,1,0:T(8,128)(2,1)}, u32[]{:S(2)}, u32[]{:S(2)}) async-start(bf16[32,2,128,256]{3,2,1,0:T(8,128)(2,1)} %bitcast.95), calls=%async_computation.1 | async-start | bytes 8388608 | tf_op jit(solution)/shard_map/all_to_all | solution.py:72
  68.8 0.0 reduce-scatter.4.cloned.1.call-start
  68.9 0.0 copy-done.5
  68.9 0.0 copy-done.6
  68.9 0.1 iota_compare_fusion.1
  69.0 0.0 copy-done.4
  69.0 0.1 select_reduce_fusion
  69.1 0.0 copy-done
  69.1 0.9 multiply_convert_fusion
  70.1 0.0 copy-start.2
  70.1 0.8 copy-done.2
  70.9 0.8 copy.32
  71.7 93.9 %all-to-all-done.1 = bf16[32,2,128,256]{3,2,1,0:T(8,128)(2,1)} async-done(((bf16[32,2,128,256]{3,2,1,0:T(8,128)(2,1)}), bf16[32,2,128,256]{3,2,1,0:T(8,128)(2,1)}, u32[]{:S(2)}, u32[]{:S(2)}) %all-to-all-start.1) | async-done | bytes 4194336 | tf_op jit(solution)/shard_map/all_to_all | solution.py:72
  165.6 7.0 %reshape.213 = bf16[8192,1,2,128]{3,2,0,1:T(2,128)(2,1)} reshape(bf16[32,2,128,256]{3,2,1,0:T(8,128)(2,1)} %all-to-all-done.1) | data formatting | bytes 8388608 | tf_op jit(solution)/shard_map/reshape | solution.py:24
  172.6 8.8 %fusion.29 = (bf16[8192,1,1,128]{3,2,0,1:T(2,128)(2,1)S(1)}, bf16[8192,1,1,128]{3,2,0,1:T(2,128)(2,1)S(1)}) fusion(bf16[8192,1,2,128]{3,2,0,1:T(2,128)(2,1)} %reshape.213), kind=kLoop, calls=%fused_computation.37 | loop fusion | bytes 8388608 | tf_op jit(solution)/shard_map/slice | solution.py:26
  181.4 1.9 copy_bitcast_fusion
  183.3 0.0 copy-start.3
  183.3 53.2 %while.10 = (s32[]{:T(128)}, f32[2,512,1,128]{3,1,2,0:T(8,128)S(1)}, bf16[2,512,1,128]{3,1,2,0:T(8,128)(2,1)}, bf16[8192,1,128]{2,0,1:T(8,128)(2,1)}, s32[2,512]...) while((s32[]{:T(128)}, ...), condition=%wide.region_2.3_spmd, body=%wide.region_1.2_spmd.sunk | while | flops 2181104128 | bytes 38444384 | solution.py:44
  183.3 0.1 compare_convert_fusion.2
  183.4 7.0 %mul.127 = f32[512,64,128]{2,1,0:T(8,128)} broadcast(f32[512,64]{1,0:T(8,128)S(1)} %compare_convert_fusion.2), dimensions={0,1} | broadcast | bytes 16908288 | tf_op jit(solution)/shard_map/while/body/eval_jaxpr/mul | solution.py:35
  190.5 19.4 %fusion.40 = f32[2,512,1,128]{3,1,2,0:T(8,128)S(1)} fusion(f32[2,512,1,128]{3,1,2,0:T(8,128)S(1)} %get-tuple-element.151, s32[]{:T(128)} %get-tuple-element.150, bf16[8192,1,128]{2,0,1:T(8,128)(2,1)S(1)} %get-tuple-element.166, f32[64,8,64,128]{3,2,1,0:T(8,128)} %bitcast.94, f32[8192]{0:T(1024)S(1)} %bitcast.105, ...), kind=kOutput, calls=%fused_computation.9.clone.1 | convolution fusion | flops 2181038080 | bytes 21398528 | tf_op jit(solution)/shard_map/while/body/eval_jaxpr/hre,ehd->rhd/dot_general | solution.py:40
  209.9 0.1 compare_convert_fusion.2
  210.1 7.0 %mul.127 = f32[512,64,128]{2,1,0:T(8,128)} broadcast(f32[512,64]{1,0:T(8,128)S(1)} %compare_convert_fusion.2), dimensions={0,1} | broadcast | bytes 16908288 | tf_op jit(solution)/shard_map/while/body/eval_jaxpr/mul | solution.py:35
  217.1 19.4 %fusion.40 = f32[2,512,1,128]{3,1,2,0:T(8,128)S(1)} fusion(f32[2,512,1,128]{3,1,2,0:T(8,128)S(1)} %get-tuple-element.151, s32[]{:T(128)} %get-tuple-element.150, bf16[8192,1,128]{2,0,1:T(8,128)(2,1)S(1)} %get-tuple-element.166, f32[64,8,64,128]{3,2,1,0:T(8,128)} %bitcast.94, f32[8192]{0:T(1024)S(1)} %bitcast.105, ...), kind=kOutput, calls=%fused_computation.9.clone.1 | convolution fusion | flops 2181038080 | bytes 21398528 | tf_op jit(solution)/shard_map/while/body/eval_jaxpr/hre,ehd->rhd/dot_general | solution.py:40
  236.5 0.2 multiply_reduce_fusion
  236.8 1.0 copy.27
  237.8 0.0 copy-done.3
  237.8 1.8 convolution_convert_fusion
  239.7 0.0 copy-start.1
  239.7 2.6 copy.28
  242.2 0.0 reduce-scatter.4.cloned.1.call-update
  242.3 30.2 %reduce-scatter.4.cloned.1.call-done = bf16[128,1024]{1,0:T(8,128)(2,1)} async-done(((bf16[1024,1024]{1,0:T(8,128)(2,1)}), bf16[128,1024]{1,0:T(8,128)(2,1)}) %reduce-scatter.4.cloned.1.call-update) | async-done | bytes 262160
  272.4 1.1 copy.29
  273.5 0.0 copy-done.1
  273.6 0.8 add_convert_fusion
  (12 shorter events, 0.1 us)
Async XLA Ops:
  6.5 62.6 %copy-start = (bf16[1024,256]{1,0:T(8,128)(2,1)S(1)}, bf16[1024,256]{1,0:T(8,128)(2,1)}, u32[]{:S(2)}) copy-start(bf16[1024,256]{1,0:T(8,128)(2,1)} %param.12) | copy-start | bytes 1572868
  9.5 20.1 %all-to-all-start.2 = ((bf16[32,2,128]{2,1,0:T(2,128)(2,1)}), bf16[32,2,128]{2,1,0:T(2,128)(2,1)S(1)}, u32[]{:S(2)}, u32[]{:S(2)}) async-start(bf16[32,2,128]{2,1,0:T(2,128)(2,1)} %bitcast.16), calls=%async_computation.2 | async-start | bytes 32768 | tf_op jit(solution)/shard_map/all_to_all | solution.py:73
  31.1 31.7 %all-to-all-start = ((bf16[8,1024,128]{1,2,0:T(8,128)(2,1)}), bf16[8,1024,128]{1,2,0:T(8,128)(2,1)S(1)}, u32[]{:S(2)}, u32[]{:S(2)}) async-start(bf16[8,1024,128]{1,2,0:T(8,128)(2,1)} %stack.2), calls=%async_computation | async-start | bytes 4194304 | tf_op jit(solution)/shard_map/all_to_all | solution.py:57
  62.8 6.1 %copy-start.5 = (s32[1024]{0:T(1024)S(1)}, s32[1024]{0:T(1024)}, u32[]{:S(2)}) copy-start(s32[1024]{0:T(1024)} %param.19) | copy-start | bytes 12292
  62.8 6.1 %copy-start.6 = (s32[8]{0:T(128)S(1)}, s32[8]{0:T(128)}, u32[]{:S(2)}) copy-start(s32[8]{0:T(128)} %param.16) | copy-start | bytes 100
  62.8 6.2 %copy-start.4 = (s32[8,8]{1,0:T(8,128)S(1)}, s32[8,8]{1,0:T(8,128)}, u32[]{:S(2)}) copy-start(s32[8,8]{1,0:T(8,128)} %param.17) | copy-start | bytes 772
  62.8 102.8 %all-to-all-start.1 = ((bf16[32,2,128,256]{3,2,1,0:T(8,128)(2,1)}), bf16[32,2,128,256]{3,2,1,0:T(8,128)(2,1)}, u32[]{:S(2)}, u32[]{:S(2)}) async-start(bf16[32,2,128,256]{3,2,1,0:T(8,128)(2,1)} %bitcast.95), calls=%async_computation.1 | async-start | bytes 8388608 | tf_op jit(solution)/shard_map/all_to_all | solution.py:72
  68.8 203.6 %reduce-scatter.4.cloned.1.call-start = ((), (), s32[]{:S(2)}) async-start(), calls=%async_computation.4 | async-start | bytes 2359296
  70.1 0.8 copy-start.2
  183.3 54.5 %copy-start.3 = (bf16[128,1024]{1,0:T(8,128)(2,1)S(1)}, bf16[128,1024]{1,0:T(8,128)(2,1)}, u32[]{:S(2)}) copy-start(bf16[128,1024]{1,0:T(8,128)(2,1)} %param.13) | copy-start | bytes 786436
  239.7 33.9 %copy-start.1 = (bf16[1024,128]{1,0:T(8,128)(2,1)S(1)}, bf16[1024,128]{1,0:T(8,128)(2,1)}, u32[]{:S(2)}) copy-start(bf16[1024,128]{1,0:T(8,128)(2,1)} %param.11) | copy-start | bytes 786436
Sparse Core Ops, SparseCore 0:
  242.4 29.9 reduce-scatter.3
